TPU v7x, 32 devices: a whole 2x2x4 slice. The times are simulated.
32 devices in a mesh: dp: 16 (over z, y, x), mp: 2 (over core).
Axes of the slice: x: 2, y: 2, z: 4, core: 2. Of those that a mesh axis runs over, the one named last changes fastest.
Arguments:
- tokens: bfloat16 [16384, 768], P(('dp', 'mp')), may hold values from -6 to 6
- seg_ids: int32 [32, 512], P('dp'), may hold values from 0 to 3, never falling along the last dimension, each value on 1 to 256 neighbouring positions
- fill_len: int32 [32], P('dp'), may hold values from 256 to 512, as said below
- qkv_weight: bfloat16 [768, 3, 768], P(None, None, 'mp'), may hold values from -0.21875 to 0.21875
- qv_bias: float32 [2, 768], P(None, 'mp'), may hold values from -3 to 3
- out_weight: bfloat16 [768, 768], replicated, may hold values from -0.875 to 0.875
- out_bias: float32 [768], replicated, may hold values from -2 to 2
- norm1_gain: float32 [768], replicated, may hold values from 0.1 to 1.9
- norm1_bias: float32 [768], replicated, may hold values from -2 to 2
- in_weight: bfloat16 [768, 3072], replicated, may hold values from -0.21875 to 0.21875
- in_bias: float32 [3072], replicated, may hold values from -3 to 3
- down_weight: bfloat16 [3072, 768], replicated, may hold values from -0.15625 to 0.15625
- down_bias: float32 [768], replicated, may hold values from -2 to 2
- norm2_gain: float32 [768], replicated, may hold values from 0.1 to 1.9
- norm2_bias: float32 [768], replicated, may hold values from -2 to 2
- act_range: float32 [4], replicated, may hold values from 1.5 to 3
- cotangent: bfloat16 [16384, 768], P(('dp', 'mp')), may hold values from -6 to 6
Outputs:
- layer_out: bfloat16 [16384, 768], P(('dp', 'mp'))
- grad_tokens: float32 [16384, 768], P(('dp', 'mp'))
- grad_qkv_weight: float32 [768, 3, 768], P(None, None, ('mp', 'dp'))
- grad_qv_bias: float32 [2, 768], P(None, ('mp', 'dp'))
- grad_out_weight: float32 [768, 768], P(('dp', 'mp'))
- grad_out_bias: float32 [768], P(('dp', 'mp'))
- grad_norm1_gain: float32 [768], P(('dp', 'mp'))
- grad_norm1_bias: float32 [768], P(('dp', 'mp'))
- grad_in_weight: float32 [768, 3072], P(('dp', 'mp'))
- grad_in_bias: float32 [3072], P(('dp', 'mp'))
- grad_down_weight: float32 [3072, 768], P(('dp', 'mp'))
- grad_down_bias: float32 [768], P(('dp', 'mp'))
- grad_norm2_gain: float32 [768], P(('dp', 'mp'))
- grad_norm2_bias: float32 [768], P(('dp', 'mp'))
- new_range: float32 [4], replicated
Inputs may be any that keep to these rules, and one draw needn't show every extreme that they name: `seg_ids`: within a packed row the document numbers never fall; each document covers 1 to 256 positions and some document covers exactly that many. `fill_len`: some packed row is full in every draw.
All inputs are finite; a program needn't handle non-finite values.
Results may differ from a plain program's by a relative error of at most 0.012.
Values may be sent and summed in bfloat16 or wider, within the bound.
A program may use at most 192 MiB of HBM per device.

v0:
```python
import functools
import math

import jax
import jax.numpy as jnp
from jax import lax
from jax.experimental import pallas as pl
from jax.experimental.pallas import tpu as pltpu
from jax.sharding import PartitionSpec as P

HD = 64
EPSILON = 1e-06
MOMENTUM = 0.9
SQRT_HALF = math.sqrt(0.5)
INV_SQRT_2PI = 1.0 / math.sqrt(2.0 * math.pi)
LOW = jnp.bfloat16
WIDE = jnp.float32
MESH = pl.DeviceIdType.MESH

MESSAGES = (
    ("down", 0, (2, 3, 1, 0)),
    ("down", 1, (1, 0, 2, 3)),
    ("down", 2, (0, 2, 3, 1)),
    ("wide", 0, (2, 0, 1, 3)),
    ("wide", 1, (1, 2, 0, 3)),
    ("wide", 2, (1, 2, 3, 0)),
    ("wide", 3, (1, 2, 3, 0)),
    ("wide", 4, (0, 1, 2, 3)),
    ("wide", 5, (0, 1, 2, 3)),
    ("wide", 6, (1, 2, 0, 3)),
    ("wide", 7, (0, 1, 2, 3)),
)
N_MSG = len(MESSAGES)
GROUPS = {"down": 0, "wide": 3}


SCHEDULE = (
    (("Dp", "Do"), 3, (
        (("Dp", 2), ((0, 0),)),
    )),
    (1, 0),
    (("Ip", "Io", "In"), 4, (
        (("Ip", 0), ((2, 0),)),
        (("Ip", 1), ((3, 0),)),
        (("Ip", 2), ((4, 0),)),
        (("Ip", 3), ((5, 0),)),
    )),
    ("LN", 0), (6, 0), (0, 1), (1, 1), ("Op", 0), (2, 1), ("Oo", 0), ("dm", 0), ("cx", 0), (7, 0),
    (("ab",), 3, (
        (("ab", 0), ((3, 1), (4, 1))),
    )),
    (("Qp",), 3, (
    )),
    (1, 2),
    (("am",), 3, (
        (("am", 0), ((5, 1), (2, 2), (0, 2))),
    )),
    (("Qo",), 3, (
        (("Qo", 0), ((8, 0),)),
        (("Qo", 1), ((9, 0), (7, 1))),
    )),
    (10, 0), ("dc", 0), (4, 2), ("sm", 0), (3, 2), (6, 1), (1, 3), ("tk", 0), (0, 3), (5, 2), (8, 1), (2, 3), (9, 1), (6, 2), (1, 4),
    (7, 2), (10, 1), (3, 3), (4, 3), (5, 3), ("sm", 1), (9, 2), (0, 4), (8, 2), (2, 4), (7, 3), (5, 4), (6, 3), (10, 2), (3, 4), (9, 3),
    ("sm", 2), (4, 4), (8, 3), (6, 4), (7, 4), (10, 3), ("sm", 3), (9, 4), (8, 4), (10, 4), ("sm", 4),
)


def dot(a, b):
    return lax.dot_general(a, b, (((1,), (0,)), ((), ())), preferred_element_type=WIDE)


def dot_nt(a, b):
    return lax.dot_general(a, b, (((1,), (1,)), ((), ())), preferred_element_type=WIDE)


def dot_tn(a, b):
    return lax.dot_general(a, b, (((0,), (0,)), ((), ())), preferred_element_type=WIDE)


def place(chunk, order):
    spot = 0
    for bit in order:
        spot = spot * 2 + (chunk >> bit) % 2
    return spot


class Scatter:
    def __init__(self, n_low, acc, csend, crecv, recvs, send_sem, recv_sem):
        self.acc, self.csend, self.crecv, self.recvs = acc, csend, crecv, recvs
        self.send_sem, self.recv_sem = send_sem, recv_sem
        self.dp, self.mp = lax.axis_index("dp"), lax.axis_index("mp")
        self.n_low = n_low
        self.pending = []
        self.next = dict.fromkeys(range(N_MSG), 0)

    def bit(self, bit):
        return (self.dp // (self.n_low << bit)) % 2

    def partner(self, bit):
        return (self.dp + (self.n_low << bit) * (1 - 2 * self.bit(bit)), self.mp)

    def core_copy(self, group, index):
        m = GROUPS[group] + index
        return pltpu.make_async_remote_copy(
            src_ref=self.csend[group].at[index % 2],
            dst_ref=self.crecv[group].at[index],
            send_sem=self.send_sem.at[m, 0],
            recv_sem=self.recv_sem.at[m, 0],
            device_id=(self.dp, 1 - self.mp),
            device_id_type=MESH,
        )

    def base(self, m, stage):
        order = MESSAGES[m][2]
        spot = 0
        for k in range(stage):
            spot = spot + self.bit(order[k]) * (8 >> k)
        return spot

    def copy(self, m, stage):
        group, index, order = MESSAGES[m]
        count = 16 >> stage
        bit = order[stage - 1]
        start = self.base(m, stage - 1) + (1 - self.bit(bit)) * count
        return pltpu.make_async_remote_copy(
            src_ref=self.acc[group].at[index, pl.ds(start, count)],
            dst_ref=self.recvs[group][stage - 1].at[index],
            send_sem=self.send_sem.at[m, stage],
            recv_sem=self.recv_sem.at[m, stage],
            device_id=self.partner(bit),
            device_id_type=MESH,
        )

    def slot_free(self, group, index):
        if isinstance(index, int):
            if index >= 2:
                self.core_copy(group, index - 2).wait_send()
        else:
            pl.when(index >= 2)(lambda: self.core_copy(group, index - 2).wait_send())

    def add(self, m, received, from_, start, count):
        group, index, _ = MESSAGES[m]
        acc = self.acc[group]
        here = pl.ds(start, count)
        acc[index, here] = acc[index, here] + received[index, pl.ds(from_, count)]

    def step(self, m, stage, out=None):
        group, index, order = MESSAGES[m]
        assert self.next[m] == stage
        self.next[m] = stage + 1
        (self.core_copy(group, index) if stage == 0 else self.copy(m, stage)).wait_recv()
        if stage == 4:
            total = self.acc[group][index, self.base(m, 4)].astype(WIDE) + self.recvs[group][3][index, 0].astype(WIDE)
            out(total)
            return
        received = self.crecv[group] if stage == 0 else self.recvs[group][stage - 1]
        count = 8 >> stage
        base = self.base(m, stage)
        mine = self.bit(order[stage])
        self.add(m, received, (1 - mine) * count, base + (1 - mine) * count, count)
        self.copy(m, stage + 1).start()
        self.pending.append((m, stage + 1))
        self.add(m, received, mine * count, base + mine * count, count)

    def finish(self):
        for group, count in (("down", 3), ("wide", N_MSG - 3)):
            for index in (count - 2, count - 1):
                self.core_copy(group, index).wait_send()
        for m, stage in self.pending:
            self.copy(m, stage).wait_send()


def spot_of(group, index, chunk):
    if isinstance(index, int):
        return place(chunk, MESSAGES[GROUPS[group] + index][2])
    spot = 0
    for other, number, order in MESSAGES:
        if other == group:
            spot = jnp.where(index == number, place(chunk, order), spot)
    return spot


def store_chunks(ref, slot, group, index, result):
    for chunk in range(16):
        if group == "down":
            piece = result[32 * chunk : 32 * chunk + 32]
        else:
            rows, half = result[24 * chunk : 24 * chunk + 24], result.shape[1] // 2
            piece = jnp.concatenate([rows[:, :half], rows[:, half:]], axis=0)
        ref[slot, spot_of(group, index, chunk)] = piece.astype(LOW)


def interleave(ref, values):
    for part in range(2):
        flipped = values(part).T
        for core in range(2):
            groups = [flipped[24 * i : 24 * i + 24] for i in range(core, 16, 2)]
            ref[core, 192 * part : 192 * part + 192, :] = jnp.concatenate(groups, axis=0).astype(LOW)


def kernel(
    n_dp, n_low,
    tok_h, seg_v, fill_s, qkvw_h, qvb_v, outw_h, outb_v, g1_v, b1_v, inw_h, inb_v, downw_h, downb_v, g2_v, b2_v, act_v, cot_h,
    lay_h, gtok_h, gqkv, gout, gin, gdown, small_o,
    tok, cot, wqkv, qvb, wout, win, wdown, clip_in, qkv, bias, ctx, stats, mixed_t, xhat1, clip_mid, clip_mid_t, clip_act_t, slope_f, h2, d_h1, pre_s, act_s, d_pre, sm, sm_r,
    acc_d, acc_w, cs_d, cs_w, cr_d, cr_w, rd1, rd2, rd3, rd4, rw1, rw2, rw3, rw4,
    loc_sem, wsend, wrecv, msend, mrecv, ssend, srecv,
):
    dp, mp = lax.axis_index("dp"), lax.axis_index("mp")
    outb_v, g1_v, b1_v, downb_v, g2_v, b2_v = (v[...].reshape(1, -1) for v in (outb_v, g1_v, b1_v, downb_v, g2_v, b2_v))
    n_bits = n_dp.bit_length() - 1
    tokens, width = tok.shape
    hidden = win.shape[1]
    half = width // 2
    other = 1 - mp
    core_id = (dp, other)

    local = [
        pltpu.make_async_copy(src, dst, loc_sem.at[i])
        for i, (src, dst) in enumerate(
            ((tok_h, tok), (qkvw_h, wqkv.at[mp]), (outw_h, wout), (inw_h, win), (downw_h, wdown), (cot_h, cot))
        )
    ]
    for copy in local[:2]:
        copy.start()
    open_ = dict(enumerate(local))
    def take(i):
        open_.pop(i).wait()

    def dp_partner(b):
        return (dp + (1 << b) * (1 - 2 * ((dp // (1 << b)) % 2)), mp)

    barrier = pltpu.get_barrier_semaphore()
    partners = [core_id] + [dp_partner(b) for b in range(n_bits)]
    for there in partners:
        pl.semaphore_signal(barrier, inc=1, device_id=there, device_id_type=MESH)

    r0, r1, r2, r3 = (act_v[0:1, i : i + 1] for i in range(4))
    i0, i1, i2, i3 = (1.0 / r for r in (r0, r1, r2, r3))

    qvb[mp] = qvb_v[...]
    take(0)
    rb = 64
    def rows_at(i, size=rb):
        return pl.ds(pl.multiple_of(i * size, size), size)

    def clip_rows(i, peak):
        v = tok[rows_at(i), :].astype(WIDE)
        clip_in[rows_at(i), :] = (r0 * jnp.tanh(v * i0)).astype(LOW)
        return jnp.maximum(peak, jnp.max(jnp.abs(v), axis=0, keepdims=True))

    peak0 = lax.fori_loop(0, tokens // rb, clip_rows, jnp.zeros((1, width), WIDE), unroll=4)
    stats[...] = jnp.zeros_like(stats)
    lane = lax.broadcasted_iota(jnp.int32, (1, 128), 1)
    in_head = [lane < HD, lane >= HD]
    qb = 256

    def project(part):
        for j in range(3):
            out = dot(clip_in[...], wqkv[part, j])
            if j == 0:
                out = (out + qvb[part, 0:1, :]).astype(LOW).astype(WIDE) * (HD ** -0.5)
            elif j == 2:
                out = out + qvb[part, 1:2, :]
            qkv[j, part] = out.astype(LOW)

    def attend(part):
        def pair(t, carry):
            at = pl.ds(pl.multiple_of(t * 128, 128), 128)
            k, v = qkv[1, part, :, at], qkv[2, part, :, at]
            nil, one = jnp.zeros_like(v), jnp.ones_like(v)
            kz = [jnp.where(m, k, nil) for m in in_head]
            vz = [jnp.concatenate([jnp.where(m, v, nil), jnp.where(m, one, nil)], axis=1) for m in in_head]
            vz = jnp.concatenate(vz, axis=0)
            head = part * 6 + t * 2
            for i in range(tokens // qb):
                rows = pl.ds(i * qb, qb)
                q = qkv[0, part, rows, at]
                es, tops = [], []
                for h in range(2):
                    s = dot_nt(q, kz[h]) + bias[rows, :]
                    tops.append(jnp.max(s, axis=-1, keepdims=True))
                    es.append(jnp.exp(s - tops[h]).astype(LOW))
                both = dot(jnp.concatenate(es, axis=1), vz)
                norm = both[:, 128:]
                ctx[rows, pl.ds(pl.multiple_of(part * half + t * 128, 128), 128)] = both[:, :128] / norm
                total = jnp.where(in_head[0], tops[0], tops[1]) + jnp.log(norm)
                found = jnp.where(lane == head, total[:, 0:1], stats[rows, :])
                stats[rows, :] = jnp.where(lane == head + 1, total[:, HD : HD + 1], found)
            return carry

        lax.fori_loop(0, half // 128, pair, 0, unroll=True)

    take(1)
    project(mp)
    pl.semaphore_wait(barrier, len(partners))
    weight_copies = [
        pltpu.make_async_remote_copy(
            src_ref=src, dst_ref=dst, send_sem=wsend.at[i], recv_sem=wrecv.at[i], device_id=core_id, device_id_type=MESH
        )
        for i, (src, dst) in enumerate(((qkvw_h, wqkv.at[mp]), (qvb_v, qvb.at[mp])))
    ]
    for copy in weight_copies:
        copy.start()
    open_["w0"], open_["w1"] = weight_copies
    for copy in local[2:]:
        copy.start()
    row = jnp.sum(jnp.where(lax.broadcasted_iota(jnp.int32, seg_v.shape, 0) == mp, seg_v[...], 0), axis=0, keepdims=True).astype(WIDE)
    fill = fill_s[mp]
    seg_col = jnp.broadcast_to(row, (128, tokens)).T[:, 0:1]
    blk = 128

    for i in range(tokens // blk):
        kpos = lax.broadcasted_iota(jnp.int32, (blk, tokens), 1)
        qpos = lax.broadcasted_iota(jnp.int32, (blk, tokens), 0) + i * blk
        live = (kpos < fill) | (kpos == qpos)
        same = seg_col[i * blk : i * blk + blk] == row
        bias[i * blk : i * blk + blk, :] = jnp.where(same & live, 0.0, -1e30)

    attend(mp)
    take("w0")
    take("w1")
    project(other)
    attend(other)

    take(2)

    def mix_rows(i, peak):
        c = ctx[rows_at(i), :]
        clip_mid[rows_at(i), :] = (r1 * jnp.tanh(c * i1)).astype(LOW)
        return jnp.maximum(peak, jnp.max(jnp.abs(c), axis=0, keepdims=True))

    peak1 = lax.fori_loop(0, tokens // rb, mix_rows, jnp.zeros((1, width), WIDE), unroll=4)
    interleave(mixed_t, lambda part: clip_mid[:, half * part : half * part + half].astype(WIDE))
    h2[...] = dot(clip_mid[...], wout[...])

    def norm(v):
        center = v - jnp.mean(v, axis=-1, keepdims=True)
        inv = lax.rsqrt(jnp.mean(center * center, axis=-1, keepdims=True) + EPSILON)
        return center * inv, inv

    def norm1_rows(i, peak):
        rows = rows_at(i)
        xhat, inv = norm(tok[rows, :].astype(WIDE) + (h2[rows, :] + outb_v))
        xhat1[rows, :] = xhat
        stats[rows, :] = jnp.where(lane == 127, inv, stats[rows, :])
        normed = xhat * g1_v + b1_v
        h2[rows, :] = normed + downb_v
        clip_mid[rows, :] = (r2 * jnp.tanh(normed * i2)).astype(LOW)
        return jnp.maximum(peak, jnp.max(jnp.abs(normed), axis=0, keepdims=True))

    peak2 = lax.fori_loop(0, tokens // rb, norm1_rows, jnp.zeros((1, width), WIDE), unroll=4)
    interleave(clip_mid_t, lambda part: clip_mid[:, half * part : half * part + half].astype(WIDE))

    take(3)
    take(4)
    fb, fr = pre_s.shape[2], 32
    n_fb = hidden // fb

    def feed_in(b):
        pre_s[b % 2] = dot(clip_mid[...], win[:, fb * b : fb * b + fb])

    def feed_act(b, peak):
        cols = slice(fb * b, fb * b + fb)
        for r in range(0, tokens, fr):
            rows = slice(r, r + fr)
            pre = pre_s[b % 2, rows, :] + inb_v[:, cols]
            cdf = 0.5 + 0.5 * lax.erf(pre * SQRT_HALF)
            act = pre * cdf
            th = jnp.tanh(act * i3)
            act_s[b % 2, rows, :] = (r3 * th).astype(LOW)
            bell = jnp.exp(pre * pre * -0.5) * INV_SQRT_2PI
            slope_f[rows, cols] = ((1.0 - th * th) * (cdf + pre * bell)).astype(LOW)
            peak = jnp.maximum(peak, jnp.max(jnp.abs(act), axis=0, keepdims=True))
        return peak

    def feed_out(b):
        out = act_s[b % 2]
        flipped = out.T
        for i in range(fb // 32):
            group = b * (fb // 32) + i
            owner = group // 3
            clip_act_t[owner % 2, group % 3, owner // 2] = flipped[32 * i : 32 * i + 32]
        h2[...] += dot(out, wdown[fb * b : fb * b + fb, :])

    peak3 = jnp.zeros((1, fb), WIDE)
    feed_in(0)
    for b in range(n_fb):
        if b + 1 < n_fb:
            feed_in(b + 1)
        peak3 = feed_act(b, peak3)
        if b > 0:
            feed_out(b - 1)
    feed_out(n_fb - 1)

    take(5)
    zero_row = jnp.zeros((1, width), WIDE)

    def norm2_rows(i, sums):
        rows = rows_at(i)
        xhat, inv = norm(h2[rows, :])
        e = cot[rows, :].astype(WIDE)
        clip_in_row = (xhat * g2_v + b2_v).astype(LOW)
        clip_mid[rows, :] = clip_in_row
        w = e * g2_v
        d = inv * (w - jnp.mean(w, axis=-1, keepdims=True) - xhat * jnp.mean(w * xhat, axis=-1, keepdims=True))
        h2[rows, :] = d
        low = d.astype(LOW)
        cot[rows, :] = low
        return (
            sums[0] + jnp.sum(e * xhat, axis=0, keepdims=True),
            sums[1] + jnp.sum(e, axis=0, keepdims=True),
            sums[2] + jnp.sum(low.astype(WIDE), axis=0, keepdims=True),
        )

    gain2, shift2, down_bias = lax.fori_loop(0, tokens // rb, norm2_rows, (zero_row, zero_row, zero_row), unroll=4)
    lay_copy = pltpu.make_async_copy(clip_mid, lay_h, loc_sem.at[6])
    lay_copy.start()

    sm[...] = jnp.zeros_like(sm)
    sm[7:8, :] = down_bias
    sm[8:9, :] = gain2
    sm[9:10, :] = shift2
    lane_w = lax.broadcasted_iota(jnp.int32, (1, width), 1)
    peaks = zero_row
    for i, peak in enumerate((peak0, peak1, peak2, peak3)):
        peaks = jnp.where(lane_w == i, jnp.max(peak, axis=-1, keepdims=True), peaks)
    sm[12:13, :] = peaks

    scatter = Scatter(
        n_low,
        {"down": acc_d, "wide": acc_w},
        {"down": cs_d, "wide": cs_w},
        {"down": cr_d, "wide": cr_w},
        {"down": (rd1, rd2, rd3, rd4), "wide": (rw1, rw2, rw3, rw4)},
        msend,
        mrecv,
    )

    def out_down(index):
        def write(total):
            gdown[32 * index : 32 * index + 32, :] = total
        return write

    def out_wide(ref, at):
        def write(total):
            both = jnp.concatenate([total[:24], total[24:]], axis=1)
            if ref is gqkv:
                ref[at] = both
            else:
                ref[:, width * at : width * at + width] = both
        return write

    outs = [out_down(i) for i in range(3)] + [out_wide(gin, i) for i in range(4)] + [out_wide(gout, 0)] + [out_wide(gqkv, i) for i in range(3)]

    def step(m, stage):
        scatter.step(m, stage, outs[m])

    def send_part(group, index, result):
        scatter.slot_free(group, index)
        store_chunks(cs_d if group == "down" else cs_w, index % 2, group, index, result)
        scatter.core_copy(group, index).start()

    def own_part(group, index, result):
        store_chunks(acc_d if group == "down" else acc_w, index, group, index, result)

    def down_send(i):
        send_part("down", i, dot(clip_act_t[other, i].reshape(16 * 32, tokens), cot[...]))

    def down_own(i):
        own_part("down", i, dot(clip_act_t[mp, i].reshape(16 * 32, tokens), cot[...]))

    def block(i):
        return pl.ds(pl.multiple_of(i * width, width), width)

    def in_send(i):
        d_pre[...] = (dot_nt(cot[...], wdown[block(i), :]) * slope_f[:, block(i)].astype(WIDE)).astype(LOW)
        send_part("wide", i, dot(clip_mid_t[other], d_pre[...]))

    def in_own(i):
        own_part("wide", i, dot(clip_mid_t[mp], d_pre[...]))
        sm[pl.ds(3 + i, 1), :] = jnp.sum(d_pre[...].astype(WIDE), axis=0, keepdims=True)

    def in_back(i):
        d_h1[...] += dot_nt(d_pre[...], win[:, block(i)])

    def norm1_back(_):
        def some(i, sums):
            rows = rows_at(i)
            xhat = xhat1[rows, :]
            inv = stats[rows, 127:128]
            th = jnp.tanh((xhat * g1_v + b1_v) * i2)
            e = h2[rows, :] + d_h1[rows, :] * (1.0 - th * th)
            w = e * g1_v
            d = inv * (w - jnp.mean(w, axis=-1, keepdims=True) - xhat * jnp.mean(w * xhat, axis=-1, keepdims=True))
            d_h1[rows, :] = d
            low = d.astype(LOW)
            cot[rows, :] = low
            return (
                sums[0] + jnp.sum(e * xhat, axis=0, keepdims=True),
                sums[1] + jnp.sum(e, axis=0, keepdims=True),
                sums[2] + jnp.sum(low.astype(WIDE), axis=0, keepdims=True),
            )

        gain1, shift1, out_bias = lax.fori_loop(0, tokens // rb, some, (zero_row, zero_row, zero_row), unroll=4)
        sm[0:1, :] = out_bias
        sm[1:2, :] = gain1
        sm[2:3, :] = shift1

    def out_send(_):
        send_part("wide", 4, dot(mixed_t[other], cot[...]))

    def out_own(_):
        own_part("wide", 4, dot(mixed_t[mp], cot[...]))

    def mixed_back(_):
        h2[...] = dot_nt(cot[...], wout[...])

    def context_back(_):
        lay_copy.wait()
        def some(i, carry):
            rows = rows_at(i)
            th = jnp.tanh(ctx[rows, :] * i1)
            clip_mid[rows, :] = (h2[rows, :].astype(LOW).astype(WIDE) * (1.0 - th * th)).astype(LOW)
            return carry

        lax.fori_loop(0, tokens // rb, some, 0, unroll=4)

    def attend_back(part, t):
        at = pl.ds(pl.multiple_of(t * 128, 128), 128)
        wide_at = pl.ds(pl.multiple_of(part * half + t * 128, 128), 128)
        k, v = qkv[1, part, :, at], qkv[2, part, :, at]
        split = lambda v: [jnp.where(m, v, jnp.zeros_like(v)) for m in in_head]
        kz, vz = split(k), split(v)
        d_k, d_v = jnp.zeros((tokens, 128), WIDE), jnp.zeros((tokens, 128), WIDE)
        for i in range(tokens // qb):
            rows = pl.ds(i * qb, qb)
            q = qkv[0, part, rows, at]
            dc = clip_mid[rows, wide_at]
            prod = dc.astype(WIDE) * ctx[rows, wide_at]
            found = stats[rows, :]
            ps, ds = [], []
            for h in range(2):
                mean = jnp.sum(jnp.where(in_head[h], prod, 0.0), axis=-1, keepdims=True)
                total = jnp.sum(jnp.where(lane == (part * 6 + t * 2 + h), found, 0.0), axis=-1, keepdims=True)
                p = jnp.exp(dot_nt(q, kz[h]) + bias[rows, :] - total)
                ds.append((p * (dot_nt(dc, vz[h]) - mean)).astype(LOW))
                ps.append(p.astype(LOW))
            d_q = dot(jnp.concatenate(ds, axis=1), jnp.concatenate(kz, axis=0))
            d_k = d_k + dot_tn(jnp.concatenate(ds, axis=0), jnp.concatenate(split(q), axis=0))
            d_v = d_v + dot_tn(jnp.concatenate(ps, axis=0), jnp.concatenate(split(dc), axis=0))
            qkv[0, part, rows, at] = (d_q * (HD ** -0.5)).astype(LOW)
        qkv[1, part, :, at] = d_k.astype(LOW)
        qkv[2, part, :, at] = d_v.astype(LOW)

    def qkv_send(j):
        send_part("wide", 5 + j, dot_tn(qkv[j, other], clip_in[...]))

    def qkv_own(j):
        own_part("wide", 5 + j, dot_tn(qkv[j, mp], clip_in[...]))

    def in_tokens(_):
        for r, j in ((10, 0), (11, 2)):
            for part in range(2):
                sm[r : r + 1, half * part : half * part + half] = jnp.sum(qkv[j, part].astype(WIDE), axis=0, keepdims=True)
        small_copy(0).start()
        h2[...] = jnp.zeros_like(h2)

        def some(n, carry):
            h2[...] += dot_nt(qkv[n % 3, n // 3], wqkv[n // 3, n % 3])
            return carry

        lax.fori_loop(0, 6, some, 0)

    def token_grad(_):
        def some(i, carry):
            rows = rows_at(i)
            th = jnp.tanh(tok[rows, :].astype(WIDE) * i0)
            d_h1[rows, :] += h2[rows, :] * (1.0 - th * th)
            return carry

        lax.fori_loop(0, tokens // rb, some, 0, unroll=4)
        tok_copy.start()

    tok_copy = pltpu.make_async_copy(d_h1, gtok_h, loc_sem.at[7])
    is_peak = lax.broadcasted_iota(jnp.int32, sm.shape, 0) == 12

    def small_copy(k):
        return pltpu.make_async_remote_copy(
            src_ref=sm,
            dst_ref=sm_r.at[k],
            send_sem=ssend.at[k],
            recv_sem=srecv.at[k],
            device_id=partners[k],
            device_id_type=MESH,
        )

    def small_end(k):
        small_copy(k).wait()
        sm[...] = jnp.where(is_peak, jnp.maximum(sm[...], sm_r[k]), sm[...] + sm_r[k])
        if k + 1 < len(partners):
            small_copy(k + 1).start()

    parts = {
        "Dp": down_send, "Do": down_own, "Ip": in_send, "Io": in_own, "In": in_back, "LN": norm1_back, "Op": out_send, "Oo": out_own,
        "dm": mixed_back, "cx": context_back, "ab": lambda t: attend_back(other, t), "am": lambda t: attend_back(mp, t),
        "Qp": qkv_send, "Qo": qkv_own, "dc": in_tokens, "tk": token_grad, "sm": small_end,
    }
    d_h1[...] = jnp.zeros_like(d_h1)

    def loop(names, count, after):
        def round_(i, carry):
            for name in names:
                parts[name](i)
                for k in range(count):
                    todo = after.get((name, k), ())
                    if todo:
                        pl.when(i == k)(lambda todo=todo: [step(*which) for which in todo] and None)
            return carry

        lax.fori_loop(0, count, round_, 0)

    for entry in SCHEDULE:
        if len(entry) == 3:
            loop(entry[0], entry[1], dict(entry[2]))
        elif isinstance(entry[0], str):
            parts[entry[0]](entry[1])
        else:
            step(*entry)
    for k in range(5, len(partners)):
        small_end(k)
    scatter.finish()

    per = width // (2 * n_dp)
    me = dp * 2 + mp
    sums = sm[...]
    out = pltpu.roll(sums, (width - per * me) % width, 1)[:, :128]
    qv_out = pltpu.roll(sums, (width - (mp * half + per * dp)) % width, 1)[:, :128]
    wide_at = 4 * per * me
    in_rows = pltpu.roll(sums, (width - wide_at % width) % width, 1)[:, :128]
    r_iota = lax.broadcasted_iota(jnp.int32, out.shape, 0)
    in_row = jnp.sum(jnp.where(r_iota == 3 + wide_at // width, in_rows, 0.0), axis=0, keepdims=True)
    out = jnp.where((r_iota == 10) | (r_iota == 11), qv_out, out)
    out = jnp.where(r_iota == 3, in_row, out)
    small_o[...] = out
    small_o[12:13, 0:4] = MOMENTUM * act_v[...] + (1.0 - MOMENTUM) * sums[12:13, 0:4]
    tok_copy.wait()


def hand_out(per, *refs):
    big, small, outs, held, sem = refs[:6], refs[6], refs[7:22], refs[22:28], refs[28]
    ins = [pltpu.make_async_copy(src, mid, sem.at[0, i]) for i, (src, mid) in enumerate(zip(big, held))]
    away = [pltpu.make_async_copy(mid, dst, sem.at[1, i]) for i, (mid, dst) in enumerate(zip(held, outs))]
    for copy in ins:
        copy.start()
    outs[6][...] = small[10:12, :per]
    for ref, row in zip(outs[7:], (0, 1, 2, 3, 7, 8, 9, 12)):
        ref[...] = small[row, : ref.shape[0]]
    for here, there in zip(ins, away):
        here.wait()
        there.start()
    for copy in away:
        copy.wait()


def per_device(n_dp, tokens, seg_ids, fill_len, qkv_weight, qv_bias, out_weight, out_bias, norm1_gain, norm1_bias, in_weight, in_bias,
               down_weight, down_bias, norm2_gain, norm2_bias, act_range, cotangent):
    n_tok, width = tokens.shape
    hidden = in_weight.shape[1]
    half = width // 2
    n_low = max(1, n_dp // 16)
    any_, vmem = pl.BlockSpec(memory_space=pl.ANY), pl.BlockSpec(memory_space=pltpu.VMEM)
    smem = pl.BlockSpec(memory_space=pltpu.SMEM)
    chunk = width // 32
    shape = jax.ShapeDtypeStruct
    low = lambda *s: pltpu.VMEM(s, LOW)
    wide = lambda *s: pltpu.VMEM(s, WIDE)
    dma = lambda *s: pltpu.SemaphoreType.DMA(s)
    n_partners = n_dp.bit_length()
    n_wide = N_MSG - 3
    outs = pl.pallas_call(
        functools.partial(kernel, n_dp, n_low),
        out_shape=(
            shape((n_tok, width), LOW),
            shape((n_tok, width), WIDE),
            shape((3, chunk, width), WIDE),
            shape((chunk, width), WIDE),
            shape((chunk, hidden), WIDE),
            shape((4 * chunk, width), WIDE),
            shape((16, 128), WIDE),
        ),
        in_specs=[any_, vmem, smem, any_, vmem, any_, vmem, vmem, vmem, any_, vmem, any_, vmem, vmem, vmem, vmem, any_],
        out_specs=(any_, any_, vmem, vmem, vmem, vmem, vmem),
        scratch_shapes=[
            low(n_tok, width), low(n_tok, width), low(2, 3, width, half), wide(2, 2, half), low(width, width), low(width, hidden), low(hidden, width),
            low(n_tok, width), low(3, 2, n_tok, half), wide(n_tok, n_tok), wide(n_tok, width), wide(n_tok, 128), low(2, half, n_tok),
            wide(n_tok, width), low(n_tok, width), low(2, half, n_tok), low(2, 3, 16, 32, n_tok), low(n_tok, hidden),
            wide(n_tok, width), wide(n_tok, width), wide(2, n_tok, 512), low(2, n_tok, 512), low(n_tok, width), wide(16, width), wide(n_partners, 16, width),
            low(3, 16, 32, width), low(n_wide, 16, 48, half), low(2, 16, 32, width), low(2, 16, 48, half), low(3, 16, 32, width), low(n_wide, 16, 48, half),
            *(low(3, 16 >> k, 32, width) for k in range(1, 5)), *(low(n_wide, 16 >> k, 48, half) for k in range(1, 5)),
            dma(8), dma(2), dma(2), dma(N_MSG, 5), dma(N_MSG, 5), dma(n_partners), dma(n_partners),
        ],
        compiler_params=pltpu.CompilerParams(collective_id=0, has_side_effects=True, vmem_limit_bytes=64 * 2**20 - 2**16),
        cost_estimate=pl.CostEstimate(flops=25_000_000_000, bytes_accessed=24_000_000, transcendentals=12_000_000),
    )(
        tokens, seg_ids, fill_len, jnp.transpose(qkv_weight, (1, 0, 2)), qv_bias, out_weight, out_bias, norm1_gain,
        norm1_bias, in_weight, in_bias.reshape(1, hidden), down_weight, down_bias, norm2_gain,
        norm2_bias, act_range.reshape(1, 4), cotangent,
    )
    layer_out, grad_tokens, qkv_sum, sum_out, sum_in, sum_down, small = outs
    if n_low > 1:
        groups = [[top * n_low + low_ for low_ in range(n_low)] for top in range(16)]
        moves = [((top * n_low + i) * 2 + core, n_low * (2 * top + core) + i) for top in range(16) for i in range(n_low) for core in range(2)]

        def spread(v, dim):
            return lax.psum_scatter(v, "dp", scatter_dimension=dim, axis_index_groups=groups, tiled=True)

        qkv_sum = spread(qkv_sum, 1)
        sum_out, sum_in, sum_down = (lax.ppermute(spread(v, 0), ("dp", "mp"), moves) for v in (sum_out, sum_in, sum_down))
    per = width // (2 * n_dp)
    rows = (per, per, per, 4 * per, per, per, per)
    vectors = [shape((size,), WIDE) for size in rows]
    big = (layer_out, grad_tokens, qkv_sum, sum_out, sum_in, sum_down)
    done = pl.pallas_call(
        functools.partial(hand_out, per),
        out_shape=(*(shape(v.shape, v.dtype) for v in big), shape((2, per), WIDE), *vectors, shape((4,), WIDE)),
        in_specs=[any_] * len(big) + [vmem],
        out_specs=(*([any_] * len(big)), *([vmem] * 9)),
        scratch_shapes=[*(pltpu.VMEM(v.shape, v.dtype) for v in big), dma(2, len(big))],
        compiler_params=pltpu.CompilerParams(vmem_limit_bytes=64 * 2**20 - 2**16),
    )(*big, small)
    layer_out, grad_tokens, qkv_sum, sum_out, sum_in, sum_down, sum_qv, out_b, gain1, shift1, in_b, down_b, gain2, shift2, new_range = done
    qkv_sum = jnp.transpose(qkv_sum, (2, 0, 1))
    return (
        layer_out, grad_tokens, qkv_sum, sum_qv, sum_out, out_b, gain1, shift1, sum_in, in_b, sum_down, down_b, gain2, shift2, new_range,
    )


def solution(mesh):
    n_dp = mesh.shape["dp"]
    both, copies = P(("dp", "mp")), P()
    rows = P(("dp", "mp"), None)
    return jax.shard_map(
        functools.partial(per_device, n_dp),
        mesh=mesh,
        in_specs=(
            rows, P("dp", None), P("dp"), P(None, None, "mp"), P(None, "mp"),
            *([copies] * 11), rows,
        ),
        out_specs=(
            rows, rows, P(None, None, ("mp", "dp")), P(None, ("mp", "dp")), rows, both, both, both, rows, both, rows, both, both, both, copies,
        ),
        check_vma=False,
    )
```

profile of v0, /device:TPU:0, one launch (start us, length us, event | category | flops | bytes accessed | tf_op | source)
XLA Modules:
  0.0 103.2 jit_solution(6274507125773404882)
XLA Ops:
  0.7 97.9 %shard_map.280 = (bf16[512,768]{1,0:T(8,128)(2,1)}, f32[512,768]{1,0:T(8,128)}, f32[3,24,768]{2,1,0:T(8,128)}, f32[24,768]{1,0:T(8,128)}, f32[24,3072]{1,0:T(8,1...) custom-call(bf16[512,768]{1,0:T(8,128)(2,1)} %tok_h.1, s32[2,512]{1,0:T(2,128)} %seg_v.1, s32[2]{0:T(128)} %fill_s.1, ...), custom_call_target="tpu_custom_call" | custom-call | flops 24999999488 | bytes 24000000 | tf_op jit(solution)/shard_map/pallas_call | solution.py:681
  98.5 4.5 %shard_map.281 = (bf16[512,768]{1,0:T(8,128)(2,1)}, f32[512,768]{1,0:T(8,128)}, f32[3,24,768]{2,1,0:T(8,128)}, f32[24,768]{1,0:T(8,128)}, f32[24,3072]{1,0:T(8,1...) custom-call(bf16[512,768]{1,0:T(8,128)(2,1)} %get-tuple-element.37.r, ...), custom_call_target="tpu_custom_call" | custom-call | tf_op jit(solution)/shard_map/pallas_call | solution.py:724
where the time goes:
time: 103 us
  Pallas kernels  102 us (99%)
    pallas_call x1, Pallas kernels, per_device(): pl.pallas_call(functools.partial(kernel, n_dp, n_low), out_shape=(shape((...  97.9 us
    pallas_call x1, Pallas kernels, per_device(): pl.pallas_call(functools.partial(hand_out, per), out_shape=(*(shape(v.sha...  4.48 us

commit v1 on v0

--- a/solution.py
+++ b/solution.py
@@ -18,50 +18,62 @@
 MESH = pl.DeviceIdType.MESH
 
 MESSAGES = (
-    ("down", 0, (2, 3, 1, 0)),
-    ("down", 1, (1, 0, 2, 3)),
-    ("down", 2, (0, 2, 3, 1)),
-    ("wide", 0, (2, 0, 1, 3)),
-    ("wide", 1, (1, 2, 0, 3)),
-    ("wide", 2, (1, 2, 3, 0)),
-    ("wide", 3, (1, 2, 3, 0)),
-    ("wide", 4, (0, 1, 2, 3)),
+    ("down", 0, (0, 1, 2, 3)),
+    ("down", 1, (2, 0, 1, 3)),
+    ("down", 2, (1, 0, 2, 3)),
+    ("wide", 0, (1, 0, 2, 3)),
+    ("wide", 1, (2, 0, 1, 3)),
+    ("wide", 2, (2, 0, 1, 3)),
+    ("wide", 3, (1, 2, 0, 3)),
+    ("wide", 4, (0, 2, 1, 3)),
     ("wide", 5, (0, 1, 2, 3)),
     ("wide", 6, (1, 2, 0, 3)),
     ("wide", 7, (0, 1, 2, 3)),
 )
 N_MSG = len(MESSAGES)
 GROUPS = {"down": 0, "wide": 3}
+SLOTS = {"down": 3, "wide": 2}
 
 
 SCHEDULE = (
-    (("Dp", "Do"), 3, (
-        (("Dp", 2), ((0, 0),)),
+    (("Dp",), 3, (
     )),
-    (1, 0),
+    (("Do",), 3, (
+        (("Do", 0), ((0, 0),)),
+        (("Do", 1), ((1, 0),)),
+    )),
     (("Ip", "Io", "In"), 4, (
         (("Ip", 0), ((2, 0),)),
-        (("Ip", 1), ((3, 0),)),
-        (("Ip", 2), ((4, 0),)),
-        (("Ip", 3), ((5, 0),)),
+        (("In", 0), ((3, 0),)),
+        (("Io", 1), ((0, 1),)),
+        (("In", 1), ((1, 1), (4, 0))),
+        (("Ip", 2), ((2, 1),)),
+        (("In", 2), ((5, 0),)),
     )),
-    ("LN", 0), (6, 0), (0, 1), (1, 1), ("Op", 0), (2, 1), ("Oo", 0), ("dm", 0), ("cx", 0), (7, 0),
+    (1, 2), (6, 0), ("LN", 0), (4, 1), ("Op", 0), ("Oo", 0), ("dm", 0), (3, 1), (2, 2), (7, 0), ("cx", 0),
     (("ab",), 3, (
-        (("ab", 0), ((3, 1), (4, 1))),
+        (("ab", 1), ((4, 2),)),
     )),
+    (5, 1), (0, 2),
     (("Qp",), 3, (
     )),
-    (1, 2),
+    (3, 2),
     (("am",), 3, (
-        (("am", 0), ((5, 1), (2, 2), (0, 2))),
+        (("am", 0), ((1, 3), (2, 3))),
+        (("am", 1), ((0, 3),)),
     )),
+    (7, 1),
     (("Qo",), 3, (
-        (("Qo", 0), ((8, 0),)),
-        (("Qo", 1), ((9, 0), (7, 1))),
+        (("Qo", 0), ((8, 0), (3, 3), (6, 1))),
+        (("Qo", 1), ((9, 0),)),
     )),
-    (10, 0), ("dc", 0), (4, 2), ("sm", 0), (3, 2), (6, 1), (1, 3), ("tk", 0), (0, 3), (5, 2), (8, 1), (2, 3), (9, 1), (6, 2), (1, 4),
-    (7, 2), (10, 1), (3, 3), (4, 3), (5, 3), ("sm", 1), (9, 2), (0, 4), (8, 2), (2, 4), (7, 3), (5, 4), (6, 3), (10, 2), (3, 4), (9, 3),
-    ("sm", 2), (4, 4), (8, 3), (6, 4), (7, 4), (10, 3), ("sm", 3), (9, 4), (8, 4), (10, 4), ("sm", 4),
+    (10, 0), ("hs", 0),
+    (("dc",), 3, (
+        (("dc", 0), (("sm", 0),)),
+    )),
+    ("tk", 0), (4, 3), (5, 2), (7, 2), (9, 1), (8, 1), (6, 2), (5, 3), ("sm", 1), (7, 3), (9, 2), (10, 1), (8, 2), ("sm", 2), (10, 2),
+    (6, 3), (8, 3), (9, 3), (10, 3), ("sm", 3), (1, 4), (2, 4), (0, 4), (3, 4), (4, 4), (5, 4), (7, 4), ("sm", 4), (6, 4), (8, 4), (9, 4),
+    (10, 4),
 )
 
 
@@ -102,10 +114,10 @@
     def core_copy(self, group, index):
         m = GROUPS[group] + index
         return pltpu.make_async_remote_copy(
-            src_ref=self.csend[group].at[index % 2],
+            src_ref=self.csend[group].at[index % SLOTS[group]],
             dst_ref=self.crecv[group].at[index],
-            send_sem=self.send_sem.at[m, 0],
-            recv_sem=self.recv_sem.at[m, 0],
+            send_sem=self.send_sem.at[m, 0, 0],
+            recv_sem=self.recv_sem.at[m, 0, 0],
             device_id=(self.dp, 1 - self.mp),
             device_id_type=MESH,
         )
@@ -117,26 +129,35 @@
             spot = spot + self.bit(order[k]) * (8 >> k)
         return spot
 
-    def copy(self, m, stage):
+    def copies(self, m, stage):
         group, index, order = MESSAGES[m]
         count = 16 >> stage
         bit = order[stage - 1]
         start = self.base(m, stage - 1) + (1 - self.bit(bit)) * count
-        return pltpu.make_async_remote_copy(
-            src_ref=self.acc[group].at[index, pl.ds(start, count)],
-            dst_ref=self.recvs[group][stage - 1].at[index],
-            send_sem=self.send_sem.at[m, stage],
-            recv_sem=self.recv_sem.at[m, stage],
-            device_id=self.partner(bit),
-            device_id_type=MESH,
-        )
+        if stage == 4:
+            parts = [(0, 1)]
+        else:
+            mine = self.bit(order[stage])
+            parts = [((1 - mine) * (count // 2), count // 2), (mine * (count // 2), count // 2)]
+        return [
+            pltpu.make_async_remote_copy(
+                src_ref=self.acc[group].at[index, pl.ds(start + first, size)],
+                dst_ref=self.recvs[group][stage - 1].at[index, pl.ds(first, size)],
+                send_sem=self.send_sem.at[m, stage, n],
+                recv_sem=self.recv_sem.at[m, stage, n],
+                device_id=self.partner(bit),
+                device_id_type=MESH,
+            )
+            for n, (first, size) in enumerate(parts)
+        ]
 
     def slot_free(self, group, index):
+        old = index - SLOTS[group]
         if isinstance(index, int):
-            if index >= 2:
-                self.core_copy(group, index - 2).wait_send()
+            if old >= 0:
+                self.core_copy(group, old).wait_send()
         else:
-            pl.when(index >= 2)(lambda: self.core_copy(group, index - 2).wait_send())
+            pl.when(old >= 0)(lambda: self.core_copy(group, old).wait_send())
 
     def add(self, m, received, from_, start, count):
         group, index, _ = MESSAGES[m]
@@ -144,30 +165,41 @@
         here = pl.ds(start, count)
         acc[index, here] = acc[index, here] + received[index, pl.ds(from_, count)]
 
+    def add_half(self, m, stage, keep):
+        group, index, order = MESSAGES[m]
+        received = self.crecv[group] if stage == 0 else self.recvs[group][stage - 1]
+        count = 8 >> stage
+        mine = self.bit(order[stage])
+        half = mine if keep else 1 - mine
+        self.add(m, received, half * count, self.base(m, stage) + half * count, count)
+
     def step(self, m, stage, out=None):
-        group, index, order = MESSAGES[m]
+        group, index, _ = MESSAGES[m]
         assert self.next[m] == stage
         self.next[m] = stage + 1
-        (self.core_copy(group, index) if stage == 0 else self.copy(m, stage)).wait_recv()
+        if stage == 0:
+            self.core_copy(group, index).wait_recv()
+        else:
+            if stage >= 2:
+                self.copies(m, stage - 1)[1].wait_recv()
+            self.add_half(m, stage - 1, True)
+            self.copies(m, stage)[0].wait_recv()
         if stage == 4:
             total = self.acc[group][index, self.base(m, 4)].astype(WIDE) + self.recvs[group][3][index, 0].astype(WIDE)
             out(total)
             return
-        received = self.crecv[group] if stage == 0 else self.recvs[group][stage - 1]
-        count = 8 >> stage
-        base = self.base(m, stage)
-        mine = self.bit(order[stage])
-        self.add(m, received, (1 - mine) * count, base + (1 - mine) * count, count)
-        self.copy(m, stage + 1).start()
+        self.add_half(m, stage, False)
+        for copy in self.copies(m, stage + 1):
+            copy.start()
         self.pending.append((m, stage + 1))
-        self.add(m, received, mine * count, base + mine * count, count)
 
     def finish(self):
         for group, count in (("down", 3), ("wide", N_MSG - 3)):
-            for index in (count - 2, count - 1):
+            for index in range(count - SLOTS[group], count):
                 self.core_copy(group, index).wait_send()
         for m, stage in self.pending:
-            self.copy(m, stage).wait_send()
+            for copy in self.copies(m, stage):
+                copy.wait_send()
 
 
 def spot_of(group, index, chunk):
@@ -200,14 +232,15 @@
 
 def kernel(
     n_dp, n_low,
-    tok_h, seg_v, fill_s, qkvw_h, qvb_v, outw_h, outb_v, g1_v, b1_v, inw_h, inb_v, downw_h, downb_v, g2_v, b2_v, act_v, cot_h,
-    lay_h, gtok_h, gqkv, gout, gin, gdown, small_o,
-    tok, cot, wqkv, qvb, wout, win, wdown, clip_in, qkv, bias, ctx, stats, mixed_t, xhat1, clip_mid, clip_mid_t, clip_act_t, slope_f, h2, d_h1, pre_s, act_s, d_pre, sm, sm_r,
+    tok_h, seg_v, fill_s, qkvw_h, qvb_v, outw_h, outb_v, g1_v, b1_v, inw_h, inb_v, downw_h, downb_v, g2_v, b2_v, act_v, range_s, cot_h,
+    lay_h, gtok_h, gqkv_h, gout_h, gin_h, gdown_h, small_o,
+    tok, cot, wqkv, qvb, wout, win, wdown, clip_in, qkv, bias, ctx, stats, mixed_t, xhat1, clip_mid, clip_mid_t, clip_act_t, slope_f, h2, d_h1, pre_b, act_a, act_b, vec_s, peak_s, sm, sm_r,
     acc_d, acc_w, cs_d, cs_w, cr_d, cr_w, rd1, rd2, rd3, rd4, rw1, rw2, rw3, rw4,
-    loc_sem, wsend, wrecv, msend, mrecv, ssend, srecv,
+    gqkv, gout, gin, gdown, out_sem, loc_sem, wsend, wrecv, msend, mrecv, ssend, srecv,
 ):
     dp, mp = lax.axis_index("dp"), lax.axis_index("mp")
-    outb_v, g1_v, b1_v, downb_v, g2_v, b2_v = (v[...].reshape(1, -1) for v in (outb_v, g1_v, b1_v, downb_v, g2_v, b2_v))
+    for i, v in enumerate((outb_v, g1_v, b1_v, downb_v, g2_v, b2_v)):
+        vec_s[i : i + 1, :] = v[...].reshape(1, -1)
     n_bits = n_dp.bit_length() - 1
     tokens, width = tok.shape
     hidden = win.shape[1]
@@ -231,16 +264,16 @@
         return (dp + (1 << b) * (1 - 2 * ((dp // (1 << b)) % 2)), mp)
 
     barrier = pltpu.get_barrier_semaphore()
-    partners = [core_id] + [dp_partner(b) for b in range(n_bits)]
+    partners = [core_id] + [dp_partner(b) for b in reversed(range(2, n_bits))] + [dp_partner(b) for b in range(2)]
     for there in partners:
         pl.semaphore_signal(barrier, inc=1, device_id=there, device_id_type=MESH)
 
-    r0, r1, r2, r3 = (act_v[0:1, i : i + 1] for i in range(4))
+    r0, r1, r2, r3 = (range_s[i] for i in range(4))
     i0, i1, i2, i3 = (1.0 / r for r in (r0, r1, r2, r3))
 
     qvb[mp] = qvb_v[...]
     take(0)
-    rb = 64
+    rb = 256
     def rows_at(i, size=rb):
         return pl.ds(pl.multiple_of(i * size, size), size)
 
@@ -249,7 +282,7 @@
         clip_in[rows_at(i), :] = (r0 * jnp.tanh(v * i0)).astype(LOW)
         return jnp.maximum(peak, jnp.max(jnp.abs(v), axis=0, keepdims=True))
 
-    peak0 = lax.fori_loop(0, tokens // rb, clip_rows, jnp.zeros((1, width), WIDE), unroll=4)
+    peak_s[0:1, :] = lax.fori_loop(0, tokens // rb, clip_rows, jnp.zeros((1, width), WIDE), unroll=4)
     stats[...] = jnp.zeros_like(stats)
     lane = lax.broadcasted_iota(jnp.int32, (1, 128), 1)
     in_head = [lane < HD, lane >= HD]
@@ -330,7 +363,7 @@
         clip_mid[rows_at(i), :] = (r1 * jnp.tanh(c * i1)).astype(LOW)
         return jnp.maximum(peak, jnp.max(jnp.abs(c), axis=0, keepdims=True))
 
-    peak1 = lax.fori_loop(0, tokens // rb, mix_rows, jnp.zeros((1, width), WIDE), unroll=4)
+    peak_s[1:2, :] = lax.fori_loop(0, tokens // rb, mix_rows, jnp.zeros((1, width), WIDE), unroll=4)
     interleave(mixed_t, lambda part: clip_mid[:, half * part : half * part + half].astype(WIDE))
     h2[...] = dot(clip_mid[...], wout[...])
 
@@ -341,41 +374,42 @@
 
     def norm1_rows(i, peak):
         rows = rows_at(i)
-        xhat, inv = norm(tok[rows, :].astype(WIDE) + (h2[rows, :] + outb_v))
+        xhat, inv = norm(tok[rows, :].astype(WIDE) + (h2[rows, :] + vec_s[0:1, :]))
         xhat1[rows, :] = xhat
         stats[rows, :] = jnp.where(lane == 127, inv, stats[rows, :])
-        normed = xhat * g1_v + b1_v
-        h2[rows, :] = normed + downb_v
+        normed = xhat * vec_s[1:2, :] + vec_s[2:3, :]
+        h2[rows, :] = normed + vec_s[3:4, :]
         clip_mid[rows, :] = (r2 * jnp.tanh(normed * i2)).astype(LOW)
         return jnp.maximum(peak, jnp.max(jnp.abs(normed), axis=0, keepdims=True))
 
-    peak2 = lax.fori_loop(0, tokens // rb, norm1_rows, jnp.zeros((1, width), WIDE), unroll=4)
+    peak_s[2:3, :] = lax.fori_loop(0, tokens // rb, norm1_rows, jnp.zeros((1, width), WIDE), unroll=1)
     interleave(clip_mid_t, lambda part: clip_mid[:, half * part : half * part + half].astype(WIDE))
 
     take(3)
     take(4)
-    fb, fr = pre_s.shape[2], 32
+    fb, fr = pre_b.shape[1], 64
+    pre_s, act_s = (d_h1.at[:, 0:fb], pre_b), (act_a, act_b)
     n_fb = hidden // fb
 
     def feed_in(b):
-        pre_s[b % 2] = dot(clip_mid[...], win[:, fb * b : fb * b + fb])
+        pre_s[b % 2][...] = dot(clip_mid[...], win[:, fb * b : fb * b + fb])
 
     def feed_act(b, peak):
         cols = slice(fb * b, fb * b + fb)
         for r in range(0, tokens, fr):
             rows = slice(r, r + fr)
-            pre = pre_s[b % 2, rows, :] + inb_v[:, cols]
+            pre = pre_s[b % 2][rows, :] + inb_v[:, cols]
             cdf = 0.5 + 0.5 * lax.erf(pre * SQRT_HALF)
             act = pre * cdf
             th = jnp.tanh(act * i3)
-            act_s[b % 2, rows, :] = (r3 * th).astype(LOW)
+            act_s[b % 2][rows, :] = (r3 * th).astype(LOW)
             bell = jnp.exp(pre * pre * -0.5) * INV_SQRT_2PI
             slope_f[rows, cols] = ((1.0 - th * th) * (cdf + pre * bell)).astype(LOW)
             peak = jnp.maximum(peak, jnp.max(jnp.abs(act), axis=0, keepdims=True))
         return peak
 
     def feed_out(b):
-        out = act_s[b % 2]
+        out = act_s[b % 2][...]
         flipped = out.T
         for i in range(fb // 32):
             group = b * (fb // 32) + i
@@ -392,6 +426,8 @@
         if b > 0:
             feed_out(b - 1)
     feed_out(n_fb - 1)
+    peak_s[3:4, :] = jnp.zeros_like(peak_s[3:4, :])
+    peak_s[3:4, 0:fb] = peak3
 
     take(5)
     zero_row = jnp.zeros((1, width), WIDE)
@@ -400,9 +436,9 @@
         rows = rows_at(i)
         xhat, inv = norm(h2[rows, :])
         e = cot[rows, :].astype(WIDE)
-        clip_in_row = (xhat * g2_v + b2_v).astype(LOW)
+        clip_in_row = (xhat * vec_s[4:5, :] + vec_s[5:6, :]).astype(LOW)
         clip_mid[rows, :] = clip_in_row
-        w = e * g2_v
+        w = e * vec_s[4:5, :]
         d = inv * (w - jnp.mean(w, axis=-1, keepdims=True) - xhat * jnp.mean(w * xhat, axis=-1, keepdims=True))
         h2[rows, :] = d
         low = d.astype(LOW)
@@ -413,7 +449,7 @@
             sums[2] + jnp.sum(low.astype(WIDE), axis=0, keepdims=True),
         )
 
-    gain2, shift2, down_bias = lax.fori_loop(0, tokens // rb, norm2_rows, (zero_row, zero_row, zero_row), unroll=4)
+    gain2, shift2, down_bias = lax.fori_loop(0, tokens // rb, norm2_rows, (zero_row, zero_row, zero_row), unroll=1)
     lay_copy = pltpu.make_async_copy(clip_mid, lay_h, loc_sem.at[6])
     lay_copy.start()
 
@@ -423,8 +459,8 @@
     sm[9:10, :] = shift2
     lane_w = lax.broadcasted_iota(jnp.int32, (1, width), 1)
     peaks = zero_row
-    for i, peak in enumerate((peak0, peak1, peak2, peak3)):
-        peaks = jnp.where(lane_w == i, jnp.max(peak, axis=-1, keepdims=True), peaks)
+    for i in range(4):
+        peaks = jnp.where(lane_w == i, jnp.max(peak_s[i : i + 1, :], axis=-1, keepdims=True), peaks)
     sm[12:13, :] = peaks
 
     scatter = Scatter(
@@ -437,28 +473,42 @@
         mrecv,
     )
 
+    leaving = []
+
+    def leave(src, dst):
+        leaving.append(pltpu.make_async_copy(src, dst, out_sem.at[len(leaving)]))
+        leaving[-1].start()
+
     def out_down(index):
         def write(total):
-            gdown[32 * index : 32 * index + 32, :] = total
+            rows = pl.ds(32 * index, 32)
+            gdown[rows, :] = total
+            leave(gdown.at[rows], gdown_h.at[rows])
+
         return write
 
-    def out_wide(ref, at):
+    def out_wide(ref, there, at):
         def write(total):
             both = jnp.concatenate([total[:24], total[24:]], axis=1)
             if ref is gqkv:
                 ref[at] = both
+                leave(ref.at[at], there.at[at])
             else:
-                ref[:, width * at : width * at + width] = both
+                cols = pl.ds(width * at, width)
+                ref[:, cols] = both
+                leave(ref.at[:, cols], there.at[:, cols])
+
         return write
 
-    outs = [out_down(i) for i in range(3)] + [out_wide(gin, i) for i in range(4)] + [out_wide(gout, 0)] + [out_wide(gqkv, i) for i in range(3)]
+    outs = [out_down(i) for i in range(3)] + [out_wide(gin, gin_h, i) for i in range(4)]
+    outs += [out_wide(gout, gout_h, 0)] + [out_wide(gqkv, gqkv_h, i) for i in range(3)]
 
     def step(m, stage):
         scatter.step(m, stage, outs[m])
 
     def send_part(group, index, result):
         scatter.slot_free(group, index)
-        store_chunks(cs_d if group == "down" else cs_w, index % 2, group, index, result)
+        store_chunks(cs_d if group == "down" else cs_w, index % SLOTS[group], group, index, result)
         scatter.core_copy(group, index).start()
 
     def own_part(group, index, result):
@@ -469,6 +519,8 @@
 
     def down_own(i):
         own_part("down", i, dot(clip_act_t[mp, i].reshape(16 * 32, tokens), cot[...]))
+
+    d_pre = clip_mid
 
     def block(i):
         return pl.ds(pl.multiple_of(i * width, width), width)
@@ -489,9 +541,9 @@
             rows = rows_at(i)
             xhat = xhat1[rows, :]
             inv = stats[rows, 127:128]
-            th = jnp.tanh((xhat * g1_v + b1_v) * i2)
+            th = jnp.tanh((xhat * vec_s[1:2, :] + vec_s[2:3, :]) * i2)
             e = h2[rows, :] + d_h1[rows, :] * (1.0 - th * th)
-            w = e * g1_v
+            w = e * vec_s[1:2, :]
             d = inv * (w - jnp.mean(w, axis=-1, keepdims=True) - xhat * jnp.mean(w * xhat, axis=-1, keepdims=True))
             d_h1[rows, :] = d
             low = d.astype(LOW)
@@ -517,7 +569,6 @@
         h2[...] = dot_nt(cot[...], wout[...])
 
     def context_back(_):
-        lay_copy.wait()
         def some(i, carry):
             rows = rows_at(i)
             th = jnp.tanh(ctx[rows, :] * i1)
@@ -559,18 +610,16 @@
     def qkv_own(j):
         own_part("wide", 5 + j, dot_tn(qkv[j, mp], clip_in[...]))
 
-    def in_tokens(_):
+    def head_sums(_):
         for r, j in ((10, 0), (11, 2)):
             for part in range(2):
                 sm[r : r + 1, half * part : half * part + half] = jnp.sum(qkv[j, part].astype(WIDE), axis=0, keepdims=True)
         small_copy(0).start()
         h2[...] = jnp.zeros_like(h2)
 
-        def some(n, carry):
-            h2[...] += dot_nt(qkv[n % 3, n // 3], wqkv[n // 3, n % 3])
-            return carry
-
-        lax.fori_loop(0, 6, some, 0)
+    def in_tokens(j):
+        both = jnp.concatenate([qkv[j, 0], qkv[j, 1]], axis=1)
+        h2[...] += dot_nt(both, jnp.concatenate([wqkv[0, j], wqkv[1, j]], axis=1))
 
     def token_grad(_):
         def some(i, carry):
@@ -583,7 +632,6 @@
         tok_copy.start()
 
     tok_copy = pltpu.make_async_copy(d_h1, gtok_h, loc_sem.at[7])
-    is_peak = lax.broadcasted_iota(jnp.int32, sm.shape, 0) == 12
 
     def small_copy(k):
         return pltpu.make_async_remote_copy(
@@ -597,16 +645,40 @@
 
     def small_end(k):
         small_copy(k).wait()
+        is_peak = lax.broadcasted_iota(jnp.int32, sm.shape, 0) == 12
         sm[...] = jnp.where(is_peak, jnp.maximum(sm[...], sm_r[k]), sm[...] + sm_r[k])
         if k + 1 < len(partners):
             small_copy(k + 1).start()
+        else:
+            small_results()
+
+    def small_results():
+        per = width // (2 * n_dp)
+        me = dp * 2 + mp
+        sums = sm[...]
+        out = pltpu.roll(sums, (width - per * me) % width, 1)[:, :128]
+        qv_out = pltpu.roll(sums, (width - (mp * half + per * dp)) % width, 1)[:, :128]
+        wide_at = 4 * per * me
+        in_rows = pltpu.roll(sums, (width - wide_at % width) % width, 1)[:, :128]
+        r_iota = lax.broadcasted_iota(jnp.int32, out.shape, 0)
+        in_row = jnp.sum(jnp.where(r_iota == 3 + wide_at // width, in_rows, 0.0), axis=0, keepdims=True)
+        out = jnp.where((r_iota == 10) | (r_iota == 11), qv_out, out)
+        out = jnp.where(r_iota == 3, in_row, out)
+        small_o[...] = out
+        small_o[12:13, 0:4] = MOMENTUM * act_v[...] + (1.0 - MOMENTUM) * sums[12:13, 0:4]
 
     parts = {
         "Dp": down_send, "Do": down_own, "Ip": in_send, "Io": in_own, "In": in_back, "LN": norm1_back, "Op": out_send, "Oo": out_own,
         "dm": mixed_back, "cx": context_back, "ab": lambda t: attend_back(other, t), "am": lambda t: attend_back(mp, t),
-        "Qp": qkv_send, "Qo": qkv_own, "dc": in_tokens, "tk": token_grad, "sm": small_end,
+        "Qp": qkv_send, "Qo": qkv_own, "hs": head_sums, "dc": in_tokens, "tk": token_grad, "sm": small_end,
     }
     d_h1[...] = jnp.zeros_like(d_h1)
+
+    def run(which, n):
+        if isinstance(which, str):
+            parts[which](n)
+        else:
+            step(which, n)
 
     def loop(names, count, after):
         def round_(i, carry):
@@ -615,42 +687,35 @@
                 for k in range(count):
                     todo = after.get((name, k), ())
                     if todo:
-                        pl.when(i == k)(lambda todo=todo: [step(*which) for which in todo] and None)
+                        pl.when(i == k)(lambda todo=todo: [run(*which) for which in todo] and None)
             return carry
 
         lax.fori_loop(0, count, round_, 0)
 
     for entry in SCHEDULE:
         if len(entry) == 3:
+            if "Ip" in entry[0]:
+                lay_copy.wait()
             loop(entry[0], entry[1], dict(entry[2]))
-        elif isinstance(entry[0], str):
-            parts[entry[0]](entry[1])
         else:
-            step(*entry)
+            run(*entry)
     for k in range(5, len(partners)):
         small_end(k)
     scatter.finish()
 
-    per = width // (2 * n_dp)
-    me = dp * 2 + mp
-    sums = sm[...]
-    out = pltpu.roll(sums, (width - per * me) % width, 1)[:, :128]
-    qv_out = pltpu.roll(sums, (width - (mp * half + per * dp)) % width, 1)[:, :128]
-    wide_at = 4 * per * me
-    in_rows = pltpu.roll(sums, (width - wide_at % width) % width, 1)[:, :128]
-    r_iota = lax.broadcasted_iota(jnp.int32, out.shape, 0)
-    in_row = jnp.sum(jnp.where(r_iota == 3 + wide_at // width, in_rows, 0.0), axis=0, keepdims=True)
-    out = jnp.where((r_iota == 10) | (r_iota == 11), qv_out, out)
-    out = jnp.where(r_iota == 3, in_row, out)
-    small_o[...] = out
-    small_o[12:13, 0:4] = MOMENTUM * act_v[...] + (1.0 - MOMENTUM) * sums[12:13, 0:4]
     tok_copy.wait()
+    for copy in leaving:
+        copy.wait()
 
 
 def hand_out(per, *refs):
     big, small, outs, held, sem = refs[:6], refs[6], refs[7:22], refs[22:28], refs[28]
-    ins = [pltpu.make_async_copy(src, mid, sem.at[0, i]) for i, (src, mid) in enumerate(zip(big, held))]
-    away = [pltpu.make_async_copy(mid, dst, sem.at[1, i]) for i, (mid, dst) in enumerate(zip(held, outs))]
+    pieces = []
+    for i, src in enumerate(big):
+        size = src.shape[0] // (4 if i < 2 else 1)
+        pieces += [(i, pl.ds(at, size)) for at in range(0, src.shape[0], size)]
+    ins = [pltpu.make_async_copy(big[i].at[at], held[i].at[at], sem.at[0, n]) for n, (i, at) in enumerate(pieces)]
+    away = [pltpu.make_async_copy(held[i].at[at], outs[i].at[at], sem.at[1, n]) for n, (i, at) in enumerate(pieces)]
     for copy in ins:
         copy.start()
     outs[6][...] = small[10:12, :per]
@@ -689,23 +754,24 @@
             shape((4 * chunk, width), WIDE),
             shape((16, 128), WIDE),
         ),
-        in_specs=[any_, vmem, smem, any_, vmem, any_, vmem, vmem, vmem, any_, vmem, any_, vmem, vmem, vmem, vmem, any_],
-        out_specs=(any_, any_, vmem, vmem, vmem, vmem, vmem),
+        in_specs=[any_, vmem, smem, any_, vmem, any_, vmem, vmem, vmem, any_, vmem, any_, vmem, vmem, vmem, vmem, smem, any_],
+        out_specs=(any_, any_, any_, any_, any_, any_, vmem),
         scratch_shapes=[
             low(n_tok, width), low(n_tok, width), low(2, 3, width, half), wide(2, 2, half), low(width, width), low(width, hidden), low(hidden, width),
             low(n_tok, width), low(3, 2, n_tok, half), wide(n_tok, n_tok), wide(n_tok, width), wide(n_tok, 128), low(2, half, n_tok),
             wide(n_tok, width), low(n_tok, width), low(2, half, n_tok), low(2, 3, 16, 32, n_tok), low(n_tok, hidden),
-            wide(n_tok, width), wide(n_tok, width), wide(2, n_tok, 512), low(2, n_tok, 512), low(n_tok, width), wide(16, width), wide(n_partners, 16, width),
-            low(3, 16, 32, width), low(n_wide, 16, 48, half), low(2, 16, 32, width), low(2, 16, 48, half), low(3, 16, 32, width), low(n_wide, 16, 48, half),
+            wide(n_tok, width), wide(n_tok, width), wide(n_tok, 512), low(n_tok, 512), low(n_tok, 512), wide(8, width), wide(8, width), wide(16, width), wide(n_partners, 16, width),
+            low(3, 16, 32, width), low(n_wide, 16, 48, half), low(3, 16, 32, width), low(2, 16, 48, half), low(3, 16, 32, width), low(n_wide, 16, 48, half),
             *(low(3, 16 >> k, 32, width) for k in range(1, 5)), *(low(n_wide, 16 >> k, 48, half) for k in range(1, 5)),
-            dma(8), dma(2), dma(2), dma(N_MSG, 5), dma(N_MSG, 5), dma(n_partners), dma(n_partners),
+            wide(3, chunk, width), wide(chunk, width), wide(chunk, hidden), wide(4 * chunk, width), dma(N_MSG),
+            dma(8), dma(2), dma(2), dma(N_MSG, 5, 2), dma(N_MSG, 5, 2), dma(n_partners), dma(n_partners),
         ],
         compiler_params=pltpu.CompilerParams(collective_id=0, has_side_effects=True, vmem_limit_bytes=64 * 2**20 - 2**16),
         cost_estimate=pl.CostEstimate(flops=25_000_000_000, bytes_accessed=24_000_000, transcendentals=12_000_000),
     )(
         tokens, seg_ids, fill_len, jnp.transpose(qkv_weight, (1, 0, 2)), qv_bias, out_weight, out_bias, norm1_gain,
         norm1_bias, in_weight, in_bias.reshape(1, hidden), down_weight, down_bias, norm2_gain,
-        norm2_bias, act_range.reshape(1, 4), cotangent,
+        norm2_bias, act_range.reshape(1, 4), act_range, cotangent,
     )
     layer_out, grad_tokens, qkv_sum, sum_out, sum_in, sum_down, small = outs
     if n_low > 1:
@@ -726,7 +792,7 @@
         out_shape=(*(shape(v.shape, v.dtype) for v in big), shape((2, per), WIDE), *vectors, shape((4,), WIDE)),
         in_specs=[any_] * len(big) + [vmem],
         out_specs=(*([any_] * len(big)), *([vmem] * 9)),
-        scratch_shapes=[*(pltpu.VMEM(v.shape, v.dtype) for v in big), dma(2, len(big))],
+        scratch_shapes=[*(pltpu.VMEM(v.shape, v.dtype) for v in big), dma(2, len(big) + 6)],
         compiler_params=pltpu.CompilerParams(vmem_limit_bytes=64 * 2**20 - 2**16),
     )(*big, small)
     layer_out, grad_tokens, qkv_sum, sum_out, sum_in, sum_down, sum_qv, out_b, gain1, shift1, in_b, down_b, gain2, shift2, new_range = done

time: 103 us -> 100 us (0.971)
  Pallas kernels: 102 us -> 98.9 us
    pallas_call x1, Pallas kernels: 97.9 us -> 94.5 us  [per_device(): pl.pallas_call(functools.partial(kernel, n_dp, n_low), out_shape=(shape((...]
where the time goes in v1:
time: 100 us; the launch traced here: 99.8 us
  Pallas kernels  98.9 us (99%)
    pallas_call x1, Pallas kernels, per_device(): pl.pallas_call(functools.partial(kernel, n_dp, n_low), out_shape=(shape((...  94.5 us
    pallas_call x1, Pallas kernels, per_device(): pl.pallas_call(functools.partial(hand_out, per), out_shape=(*(shape(v.sha...  4.46 us

profile of v1, /device:TPU:0, one launch (start us, length us, event | category | flops | bytes accessed | tf_op | source)
XLA Modules:
  0.0 99.8 jit_solution(756292105456387082)
XLA Ops:
  0.7 94.5 %shard_map.280 = (bf16[512,768]{1,0:T(8,128)(2,1)}, f32[512,768]{1,0:T(8,128)}, f32[3,24,768]{2,1,0:T(8,128)}, f32[24,768]{1,0:T(8,128)}, f32[24,3072]{1,0:T(8,1...) custom-call(bf16[512,768]{1,0:T(8,128)(2,1)} %tok_h.1, s32[2,512]{1,0:T(2,128)} %seg_v.1, s32[2]{0:T(128)} %fill_s.1, ...), custom_call_target="tpu_custom_call" | custom-call | flops 24999999488 | bytes 24000000 | tf_op jit(solution)/shard_map/pallas_call | solution.py:746
  95.1 4.5 %shard_map.281 = (bf16[512,768]{1,0:T(8,128)(2,1)}, f32[512,768]{1,0:T(8,128)}, f32[3,24,768]{2,1,0:T(8,128)}, f32[24,768]{1,0:T(8,128)}, f32[24,3072]{1,0:T(8,1...) custom-call(bf16[512,768]{1,0:T(8,128)(2,1)} %get-tuple-element.37.r, ...), custom_call_target="tpu_custom_call" | custom-call | tf_op jit(solution)/shard_map/pallas_call | solution.py:790

commit v2 on v1

--- a/solution.py
+++ b/solution.py
@@ -19,14 +19,14 @@
 
 MESSAGES = (
     ("down", 0, (0, 1, 2, 3)),
-    ("down", 1, (2, 0, 1, 3)),
-    ("down", 2, (1, 0, 2, 3)),
+    ("down", 1, (1, 2, 0, 3)),
+    ("down", 2, (2, 0, 1, 3)),
     ("wide", 0, (1, 0, 2, 3)),
-    ("wide", 1, (2, 0, 1, 3)),
-    ("wide", 2, (2, 0, 1, 3)),
-    ("wide", 3, (1, 2, 0, 3)),
-    ("wide", 4, (0, 2, 1, 3)),
-    ("wide", 5, (0, 1, 2, 3)),
+    ("wide", 1, (0, 1, 2, 3)),
+    ("wide", 2, (1, 2, 0, 3)),
+    ("wide", 3, (2, 1, 0, 3)),
+    ("wide", 4, (0, 1, 2, 3)),
+    ("wide", 5, (0, 2, 1, 3)),
     ("wide", 6, (1, 2, 0, 3)),
     ("wide", 7, (0, 1, 2, 3)),
 )
@@ -50,30 +50,29 @@
         (("Ip", 2), ((2, 1),)),
         (("In", 2), ((5, 0),)),
     )),
-    (1, 2), (6, 0), ("LN", 0), (4, 1), ("Op", 0), ("Oo", 0), ("dm", 0), (3, 1), (2, 2), (7, 0), ("cx", 0),
+    (6, 0), ("LN", 0), (4, 1), (3, 1), ("Op", 0), (1, 2), ("Oo", 0), ("dm", 0), (7, 0), ("cx", 0),
     (("ab",), 3, (
-        (("ab", 1), ((4, 2),)),
+        (("ab", 0), ((2, 2),)),
+        (("ab", 1), ((0, 2), (6, 1))),
     )),
-    (5, 1), (0, 2),
     (("Qp",), 3, (
+        (("Qp", 0), ((3, 2),)),
     )),
-    (3, 2),
     (("am",), 3, (
-        (("am", 0), ((1, 3), (2, 3))),
-        (("am", 1), ((0, 3),)),
+        (("am", 0), ((0, 3), (5, 1), (1, 3))),
+        (("am", 1), ((3, 3),)),
     )),
-    (7, 1),
     (("Qo",), 3, (
-        (("Qo", 0), ((8, 0), (3, 3), (6, 1))),
-        (("Qo", 1), ((9, 0),)),
+        (("Qo", 0), ((8, 0),)),
+        (("Qo", 1), ((9, 0), (7, 1), (4, 2))),
     )),
-    (10, 0), ("hs", 0),
+    (10, 0), (5, 2), ("hs", 0),
     (("dc",), 3, (
         (("dc", 0), (("sm", 0),)),
     )),
-    ("tk", 0), (4, 3), (5, 2), (7, 2), (9, 1), (8, 1), (6, 2), (5, 3), ("sm", 1), (7, 3), (9, 2), (10, 1), (8, 2), ("sm", 2), (10, 2),
-    (6, 3), (8, 3), (9, 3), (10, 3), ("sm", 3), (1, 4), (2, 4), (0, 4), (3, 4), (4, 4), (5, 4), (7, 4), ("sm", 4), (6, 4), (8, 4), (9, 4),
-    (10, 4),
+    (2, 3), ("tk", 0), (4, 3), (6, 2), (8, 1), ("sm", 1), (8, 2), (9, 1), (10, 1), ("sm", 2), (9, 2), (7, 2), (5, 3), (8, 3), (7, 3),
+    (6, 3), (10, 2), ("sm", 3), (9, 3), (10, 3), (0, 4), (1, 4), (3, 4), (2, 4), (4, 4), (5, 4), (8, 4), (7, 4), (6, 4), ("sm", 4),
+    (9, 4), (10, 4),
 )
 
 
@@ -233,10 +232,10 @@
 def kernel(
     n_dp, n_low,
     tok_h, seg_v, fill_s, qkvw_h, qvb_v, outw_h, outb_v, g1_v, b1_v, inw_h, inb_v, downw_h, downb_v, g2_v, b2_v, act_v, range_s, cot_h,
-    lay_h, gtok_h, gqkv_h, gout_h, gin_h, gdown_h, small_o,
+    lay_h, gtok_h, gqkv_h, gout_h, gin_h, gdown_h, small_h,
     tok, cot, wqkv, qvb, wout, win, wdown, clip_in, qkv, bias, ctx, stats, mixed_t, xhat1, clip_mid, clip_mid_t, clip_act_t, slope_f, h2, d_h1, pre_b, act_a, act_b, vec_s, peak_s, sm, sm_r,
     acc_d, acc_w, cs_d, cs_w, cr_d, cr_w, rd1, rd2, rd3, rd4, rw1, rw2, rw3, rw4,
-    gqkv, gout, gin, gdown, out_sem, loc_sem, wsend, wrecv, msend, mrecv, ssend, srecv,
+    small_o, gqkv, gout, gin, gdown, out_sem, loc_sem, wsend, wrecv, msend, mrecv, ssend, srecv,
 ):
     dp, mp = lax.axis_index("dp"), lax.axis_index("mp")
     for i, v in enumerate((outb_v, g1_v, b1_v, downb_v, g2_v, b2_v)):
@@ -666,6 +665,7 @@
         out = jnp.where(r_iota == 3, in_row, out)
         small_o[...] = out
         small_o[12:13, 0:4] = MOMENTUM * act_v[...] + (1.0 - MOMENTUM) * sums[12:13, 0:4]
+        leave(small_o, small_h)
 
     parts = {
         "Dp": down_send, "Do": down_own, "Ip": in_send, "Io": in_own, "In": in_back, "LN": norm1_back, "Op": out_send, "Oo": out_own,
@@ -709,18 +709,25 @@
 
 
 def hand_out(per, *refs):
-    big, small, outs, held, sem = refs[:6], refs[6], refs[7:22], refs[22:28], refs[28]
+    big, small_h, outs, held, short, small, sem = refs[:6], refs[6], refs[7:22], refs[22:28], refs[28:37], refs[37], refs[38]
     pieces = []
     for i, src in enumerate(big):
         size = src.shape[0] // (4 if i < 2 else 1)
         pieces += [(i, pl.ds(at, size)) for at in range(0, src.shape[0], size)]
     ins = [pltpu.make_async_copy(big[i].at[at], held[i].at[at], sem.at[0, n]) for n, (i, at) in enumerate(pieces)]
     away = [pltpu.make_async_copy(held[i].at[at], outs[i].at[at], sem.at[1, n]) for n, (i, at) in enumerate(pieces)]
+    last = len(pieces)
+    first = pltpu.make_async_copy(small_h, small, sem.at[0, last])
+    first.start()
     for copy in ins:
         copy.start()
-    outs[6][...] = small[10:12, :per]
-    for ref, row in zip(outs[7:], (0, 1, 2, 3, 7, 8, 9, 12)):
+    away += [pltpu.make_async_copy(src, dst, sem.at[1, last + n]) for n, (src, dst) in enumerate(zip(short, outs[6:]))]
+    first.wait()
+    short[0][...] = small[10:12, :per]
+    for ref, row in zip(short[1:], (0, 1, 2, 3, 7, 8, 9, 12)):
         ref[...] = small[row, : ref.shape[0]]
+    for copy in away[last:]:
+        copy.start()
     for here, there in zip(ins, away):
         here.wait()
         there.start()
@@ -755,7 +762,7 @@
             shape((16, 128), WIDE),
         ),
         in_specs=[any_, vmem, smem, any_, vmem, any_, vmem, vmem, vmem, any_, vmem, any_, vmem, vmem, vmem, vmem, smem, any_],
-        out_specs=(any_, any_, any_, any_, any_, any_, vmem),
+        out_specs=(any_,) * 7,
         scratch_shapes=[
             low(n_tok, width), low(n_tok, width), low(2, 3, width, half), wide(2, 2, half), low(width, width), low(width, hidden), low(hidden, width),
             low(n_tok, width), low(3, 2, n_tok, half), wide(n_tok, n_tok), wide(n_tok, width), wide(n_tok, 128), low(2, half, n_tok),
@@ -763,7 +770,7 @@
             wide(n_tok, width), wide(n_tok, width), wide(n_tok, 512), low(n_tok, 512), low(n_tok, 512), wide(8, width), wide(8, width), wide(16, width), wide(n_partners, 16, width),
             low(3, 16, 32, width), low(n_wide, 16, 48, half), low(3, 16, 32, width), low(2, 16, 48, half), low(3, 16, 32, width), low(n_wide, 16, 48, half),
             *(low(3, 16 >> k, 32, width) for k in range(1, 5)), *(low(n_wide, 16 >> k, 48, half) for k in range(1, 5)),
-            wide(3, chunk, width), wide(chunk, width), wide(chunk, hidden), wide(4 * chunk, width), dma(N_MSG),
+            wide(16, 128), wide(3, chunk, width), wide(chunk, width), wide(chunk, hidden), wide(4 * chunk, width), dma(N_MSG + 1),
             dma(8), dma(2), dma(2), dma(N_MSG, 5, 2), dma(N_MSG, 5, 2), dma(n_partners), dma(n_partners),
         ],
         compiler_params=pltpu.CompilerParams(collective_id=0, has_side_effects=True, vmem_limit_bytes=64 * 2**20 - 2**16),
@@ -790,9 +797,12 @@
     done = pl.pallas_call(
         functools.partial(hand_out, per),
         out_shape=(*(shape(v.shape, v.dtype) for v in big), shape((2, per), WIDE), *vectors, shape((4,), WIDE)),
-        in_specs=[any_] * len(big) + [vmem],
-        out_specs=(*([any_] * len(big)), *([vmem] * 9)),
-        scratch_shapes=[*(pltpu.VMEM(v.shape, v.dtype) for v in big), dma(2, len(big) + 6)],
+        in_specs=[any_] * (len(big) + 1),
+        out_specs=(any_,) * (len(big) + 9),
+        scratch_shapes=[
+            *(pltpu.VMEM(v.shape, v.dtype) for v in (*big, shape((2, per), WIDE), *vectors, shape((4,), WIDE), small)),
+            dma(2, len(big) + 15),
+        ],
         compiler_params=pltpu.CompilerParams(vmem_limit_bytes=64 * 2**20 - 2**16),
     )(*big, small)
     layer_out, grad_tokens, qkv_sum, sum_out, sum_in, sum_down, sum_qv, out_b, gain1, shift1, in_b, down_b, gain2, shift2, new_range = done

time: 100 us -> 97.6 us (0.976)
  Pallas kernels: 98.9 us -> 96.5 us
    pallas_call x1, Pallas kernels: 94.5 us -> 93.1 us  [per_device(): pl.pallas_call(functools.partial(kernel, n_dp, n_low), out_shape=(shape((...]
    pallas_call x1, Pallas kernels: 4.46 us -> 3.4 us  [per_device(): pl.pallas_call(functools.partial(hand_out, per), out_shape=(*(shape(v.sha...]
where the time goes in v2:
time: 97.6 us; the launch traced here: 97.3 us
  Pallas kernels  96.5 us (99%)
    pallas_call x1, Pallas kernels, per_device(): pl.pallas_call(functools.partial(kernel, n_dp, n_low), out_shape=(shape((...  93.1 us
    pallas_call x1, Pallas kernels, per_device(): pl.pallas_call(functools.partial(hand_out, per), out_shape=(*(shape(v.sha...  3.4 us

profile of v2, /device:TPU:0, one launch (start us, length us, event | category | flops | bytes accessed | tf_op | source)
XLA Modules:
  0.0 97.3 jit_solution(11491151495521931482)
XLA Ops:
  0.7 93.1 %shard_map.280 = (bf16[512,768]{1,0:T(8,128)(2,1)}, f32[512,768]{1,0:T(8,128)}, f32[3,24,768]{2,1,0:T(8,128)}, f32[24,768]{1,0:T(8,128)}, f32[24,3072]{1,0:T(8,1...) custom-call(bf16[512,768]{1,0:T(8,128)(2,1)} %tok_h.1, s32[2,512]{1,0:T(2,128)} %seg_v.1, s32[2]{0:T(128)} %fill_s.1, ...), custom_call_target="tpu_custom_call" | custom-call | flops 24999999488 | bytes 24000000 | tf_op jit(solution)/shard_map/pallas_call | solution.py:753
  93.7 3.4 %shard_map.281 = (bf16[512,768]{1,0:T(8,128)(2,1)}, f32[512,768]{1,0:T(8,128)}, f32[3,24,768]{2,1,0:T(8,128)}, f32[24,768]{1,0:T(8,128)}, f32[24,3072]{1,0:T(8,1...) custom-call(bf16[512,768]{1,0:T(8,128)(2,1)} %get-tuple-element.37.r, ...), custom_call_target="tpu_custom_call" | custom-call | tf_op jit(solution)/shard_map/pallas_call | solution.py:797

commit v3 on v2

--- a/solution.py
+++ b/solution.py
@@ -18,16 +18,16 @@
 MESH = pl.DeviceIdType.MESH
 
 MESSAGES = (
-    ("down", 0, (0, 1, 2, 3)),
-    ("down", 1, (1, 2, 0, 3)),
-    ("down", 2, (2, 0, 1, 3)),
-    ("wide", 0, (1, 0, 2, 3)),
-    ("wide", 1, (0, 1, 2, 3)),
-    ("wide", 2, (1, 2, 0, 3)),
-    ("wide", 3, (2, 1, 0, 3)),
-    ("wide", 4, (0, 1, 2, 3)),
-    ("wide", 5, (0, 2, 1, 3)),
-    ("wide", 6, (1, 2, 0, 3)),
+    ("down", 0, (2, 0, 1, 3)),
+    ("down", 1, (0, 2, 1, 3)),
+    ("down", 2, (1, 2, 0, 3)),
+    ("wide", 0, (0, 1, 2, 3)),
+    ("wide", 1, (1, 2, 0, 3)),
+    ("wide", 2, (1, 0, 2, 3)),
+    ("wide", 3, (1, 0, 2, 3)),
+    ("wide", 4, (2, 0, 1, 3)),
+    ("wide", 5, (0, 1, 2, 3)),
+    ("wide", 6, (2, 0, 1, 3)),
     ("wide", 7, (0, 1, 2, 3)),
 )
 N_MSG = len(MESSAGES)
@@ -47,32 +47,32 @@
         (("In", 0), ((3, 0),)),
         (("Io", 1), ((0, 1),)),
         (("In", 1), ((1, 1), (4, 0))),
-        (("Ip", 2), ((2, 1),)),
+        (("Io", 2), ((2, 1),)),
         (("In", 2), ((5, 0),)),
     )),
-    (6, 0), ("LN", 0), (4, 1), (3, 1), ("Op", 0), (1, 2), ("Oo", 0), ("dm", 0), (7, 0), ("cx", 0),
+    (1, 2), (6, 0), ("LN", 0), (3, 1), ("Op", 0), ("Oo", 0), ("dm", 0), (4, 1), (7, 0), (2, 2), ("cx", 0),
     (("ab",), 3, (
-        (("ab", 0), ((2, 2),)),
-        (("ab", 1), ((0, 2), (6, 1))),
+        (("ab", 1), ((0, 2), (4, 2))),
     )),
     (("Qp",), 3, (
-        (("Qp", 0), ((3, 2),)),
+        (("Qp", 1), ((5, 1), (2, 3))),
     )),
     (("am",), 3, (
-        (("am", 0), ((0, 3), (5, 1), (1, 3))),
-        (("am", 1), ((3, 3),)),
+        (("am", 0), ((4, 3), (7, 1))),
+        (("am", 1), ((1, 3),)),
     )),
+    (5, 2),
     (("Qo",), 3, (
         (("Qo", 0), ((8, 0),)),
-        (("Qo", 1), ((9, 0), (7, 1), (4, 2))),
+        (("Qo", 1), ((9, 0),)),
     )),
-    (10, 0), (5, 2), ("hs", 0),
+    (10, 0), (7, 2), ("hs", 0),
     (("dc",), 3, (
-        (("dc", 0), (("sm", 0),)),
+        (("dc", 0), ((6, 1), ("sm", 0))),
     )),
-    (2, 3), ("tk", 0), (4, 3), (6, 2), (8, 1), ("sm", 1), (8, 2), (9, 1), (10, 1), ("sm", 2), (9, 2), (7, 2), (5, 3), (8, 3), (7, 3),
-    (6, 3), (10, 2), ("sm", 3), (9, 3), (10, 3), (0, 4), (1, 4), (3, 4), (2, 4), (4, 4), (5, 4), (8, 4), (7, 4), (6, 4), ("sm", 4),
-    (9, 4), (10, 4),
+    (5, 3), ("tk", 0), (8, 1), (3, 2), (9, 1), (0, 3), (7, 3), (10, 1), ("sm", 1), (3, 3), (8, 2), ("sm", 2), (10, 2), (6, 2), (8, 3),
+    (10, 3), (9, 2), (6, 3), (9, 3), ("sm", 3), (2, 4), (4, 4), (1, 4), (5, 4), (0, 4), (7, 4), (3, 4), ("sm", 4), (8, 4), (10, 4),
+    (6, 4), (9, 4),
 )
 
 

time: 97.6 us -> 96.8 us (level)
  no operation moved by 1% of the time
where the time goes in v3:
time: 96.8 us; the launch traced here: 96.6 us
  Pallas kernels  95.7 us (99%)
    pallas_call x1, Pallas kernels, per_device(): pl.pallas_call(functools.partial(kernel, n_dp, n_low), out_shape=(shape((...  92.3 us
    pallas_call x1, Pallas kernels, per_device(): pl.pallas_call(functools.partial(hand_out, per), out_shape=(*(shape(v.sha...  3.4 us

profile of v3, /device:TPU:0, one launch (start us, length us, event | category | flops | bytes accessed | tf_op | source)
XLA Modules:
  0.0 96.6 jit_solution(15295147376948750332)
XLA Ops:
  0.7 92.3 %shard_map.280 = (bf16[512,768]{1,0:T(8,128)(2,1)}, f32[512,768]{1,0:T(8,128)}, f32[3,24,768]{2,1,0:T(8,128)}, f32[24,768]{1,0:T(8,128)}, f32[24,3072]{1,0:T(8,1...) custom-call(bf16[512,768]{1,0:T(8,128)(2,1)} %tok_h.1, s32[2,512]{1,0:T(2,128)} %seg_v.1, s32[2]{0:T(128)} %fill_s.1, ...), custom_call_target="tpu_custom_call" | custom-call | flops 24999999488 | bytes 24000000 | tf_op jit(solution)/shard_map/pallas_call | solution.py:753
  93.0 3.4 %shard_map.281 = (bf16[512,768]{1,0:T(8,128)(2,1)}, f32[512,768]{1,0:T(8,128)}, f32[3,24,768]{2,1,0:T(8,128)}, f32[24,768]{1,0:T(8,128)}, f32[24,3072]{1,0:T(8,1...) custom-call(bf16[512,768]{1,0:T(8,128)(2,1)} %get-tuple-element.37.r, ...), custom_call_target="tpu_custom_call" | custom-call | tf_op jit(solution)/shard_map/pallas_call | solution.py:797
